TPU v7x, 32 devices: a whole 2x2x4 slice. The times are simulated.
32 devices in a mesh: fsdp: 2 (over z_hi), seq: 8 (over y, x, core), tp: 2 (over z_lo).
Axes of the slice: x: 2, y: 2, z: 4 (z_hi: 2, z_lo: 2; z = z_hi * 2 + z_lo), core: 2. Of those that a mesh axis runs over, the one named last changes fastest.
Arguments:
- tokens: bfloat16 [4096, 8192], P(('fsdp', 'seq', 'tp')), may hold values from -6 to 6
- proj_mean: bfloat16 [8192, 4096], P(('fsdp', 'seq'), 'tp'), may hold values from -0.0625 to 0.0625
- proj_devs: bfloat16 [4, 8192, 4096], P(None, ('fsdp', 'seq'), 'tp'), may hold values from -0.0625 to 0.0625
- bc_mean: bfloat16 [8192, 2, 1024], P(('fsdp', 'seq'), None, 'tp'), may hold values from -0.0625 to 0.0625
- bc_devs: bfloat16 [4, 8192, 2, 1024], P(None, ('fsdp', 'seq'), None, 'tp'), may hold values from -0.0625 to 0.0625
- swag_coef: float32 [4], replicated, may hold values from -4 to 4
- dt_weight: bfloat16 [8192, 64], P(('fsdp', 'seq'), 'tp'), may hold values from -0.0625 to 0.0625
- dt_bias: float32 [64], P('tp'), may hold values from -12 to -2, as said below
- decay_rate: float32 [64], P('tp'), may hold values from 0 to 16, as said below
- skip_gain: float32 [64], P('tp'), may hold values from 0.5 to 1.5
- conv_proj: float32 [4, 4096], P(None, 'tp'), may hold values from -3 to 3
- conv_bc: float32 [4, 2, 1024], P(None, None, 'tp'), may hold values from -1.5 to 1.5
Outputs:
- ssm_out: bfloat16 [4096, 4096], P(('fsdp', 'seq'), 'tp')
Inputs may be any that keep to these rules, and one draw needn't show every extreme that they name: `dt_bias`: every bias is the inverse softplus of a positive step size. `decay_rate`: every rate is positive.
All inputs are finite; a program needn't handle non-finite values.
Results may differ from a plain program's by a relative error of at most 0.0059.
Values may be sent and summed in bfloat16 or wider, within the bound.
No kernel may reach another device: no remote copies, remote signals or barrier semaphores. Data moves between devices by JAX's collectives and lax.ppermute only.
A program may use at most 128 MiB of HBM per device.

v0:
```python
import jax
import jax.numpy as jnp
from jax import lax
from jax.sharding import PartitionSpec as P

P_SIZE = 64
N = 128
CONV = 4
SPAN = 128


def shifted(shard, axis, by):
    count = lax.axis_size(axis)
    pairs = [(i, i + by) for i in range(count) if 0 <= i + by < count]
    return lax.ppermute(shard, axis, pairs)


def prefix(part, axis, combine, identity):
    place = lax.axis_index(axis)
    gathered = jax.tree.map(lambda a: lax.all_gather(a, axis), part)
    state = jax.tree.map(lambda a, e: jnp.zeros_like(a) + jnp.asarray(e, a.dtype), part, identity)

    def one(hop, state):
        return combine(
            state, jax.tree.map(lambda a: lax.dynamic_index_in_dim(a, hop, 0, False), gathered)
        )

    return lax.fori_loop(0, place, one, state)


def sampled(mean_part, dev_part, swag_coef):
    factor = (2.0 * (dev_part.shape[0] - 1)) ** (-0.5)
    accum = mean_part.astype(jnp.float32)
    for member in range(dev_part.shape[0]):
        accum = accum + factor * swag_coef[member] * dev_part[member].astype(jnp.float32)
    return accum.astype(jnp.bfloat16)


def combine(former, latter):
    return (former[0] * latter[0], latter[0][:, None, None] * former[1] + latter[1])


def body(
    tokens,
    proj_mean,
    proj_devs,
    bc_mean,
    bc_devs,
    swag_coef,
    dt_weight,
    dt_bias,
    decay_rate,
    skip_gain,
    conv_proj,
    conv_bc,
):
    heads_here = decay_rate.shape[0]
    groups_here = bc_mean.shape[2] // N
    width_x = proj_mean.shape[1]
    width_bc = 2 * bc_mean.shape[2]
    rows_all = lax.all_gather(tokens, "tp", axis=0, tiled=True)
    tok_count = rows_all.shape[0]
    weight_x = sampled(proj_mean, proj_devs, swag_coef)
    weight_bc = sampled(bc_mean, bc_devs, swag_coef).reshape(bc_mean.shape[0], width_bc)
    weight_all = jnp.concatenate([weight_x, weight_bc], axis=1)
    projected = jnp.dot(
        rows_all,
        lax.all_gather(weight_all, ("fsdp", "seq"), axis=0, tiled=True),
        preferred_element_type=jnp.float32,
    ).astype(jnp.bfloat16)
    step_size = jax.nn.softplus(
        jnp.dot(
            rows_all,
            lax.all_gather(dt_weight, ("fsdp", "seq"), axis=0, tiled=True),
            preferred_element_type=jnp.float32,
        )
        + dt_bias
    )
    rim_rows = shifted(projected[tok_count - (CONV - 1) :], "seq", 1)
    padded = jnp.concatenate([rim_rows, projected], axis=0).astype(jnp.float32)
    kernel = jnp.concatenate([conv_proj, conv_bc.reshape(CONV, width_bc)], axis=1)
    conv_sum = kernel[0] * padded[0:tok_count]
    for offset in range(1, CONV):
        conv_sum = conv_sum + kernel[offset] * padded[offset : offset + tok_count]
    conved = jax.nn.silu(conv_sum).astype(jnp.bfloat16)
    blocks = tok_count // SPAN
    per_group = heads_here // groups_here
    values = conved[:, :width_x].reshape(blocks, SPAN, heads_here, P_SIZE)
    keys_b = conved[:, width_x : width_x + width_bc // 2].reshape(blocks, SPAN, groups_here, N)
    reads_c = conved[:, width_x + width_bc // 2 :].reshape(blocks, SPAN, groups_here, N)
    steps_b = step_size.reshape(blocks, SPAN, heads_here)
    cum_log = jnp.cumsum(-steps_b * decay_rate, axis=1)
    last_cum = cum_log[:, SPAN - 1 :, :]
    scaled = (
        values.astype(jnp.float32) * (jnp.exp(last_cum - cum_log) * steps_b)[..., None]
    ).astype(jnp.bfloat16)
    keys_h = jnp.repeat(keys_b, per_group, axis=2)
    states = jnp.einsum("bshn,bshp->bhnp", keys_h, scaled, preferred_element_type=jnp.float32)
    block_decay = jnp.exp(last_cum[:, 0, :])
    total_decay = block_decay[0]
    total_state = states[0]
    member = 1
    total_decay, total_state = combine(
        (total_decay, total_state), (block_decay[member], states[member])
    )
    incoming = prefix(
        (total_decay, total_state),
        "seq",
        combine,
        (jnp.ones((heads_here,), jnp.float32), jnp.zeros((heads_here, N, P_SIZE), jnp.float32)),
    )
    scores = jnp.einsum("bqgn,bsgn->bgqs", reads_c, keys_b, preferred_element_type=jnp.float32)
    scores = jnp.repeat(scores, per_group, axis=1)
    causal_mask = jnp.tril(jnp.ones((SPAN, SPAN), bool))
    later_cum = jnp.transpose(cum_log, (0, 2, 1))
    cum_gaps = later_cum[:, :, :, None] - later_cum[:, :, None, :]
    decays = jnp.where(causal_mask, jnp.exp(jnp.minimum(cum_gaps, 0.0)), 0.0)
    weights = (scores * decays * jnp.transpose(steps_b, (0, 2, 1))[:, :, None, :]).astype(
        jnp.bfloat16
    )
    inner_part = jnp.einsum("bhqs,bshp->bqhp", weights, values, preferred_element_type=jnp.float32)
    carried = incoming[1]
    entering = []
    for member in range(blocks):
        entering.append(carried)
        carried = block_decay[member][:, None, None] * carried + states[member]
    entering_bf = jnp.stack(entering).astype(jnp.bfloat16)
    reads_h = jnp.repeat(reads_c, per_group, axis=2)
    outer_part = jnp.exp(cum_log)[..., None] * jnp.einsum(
        "bqhn,bhnp->bqhp", reads_h, entering_bf, preferred_element_type=jnp.float32
    )
    result = inner_part + outer_part + skip_gain[:, None] * values.astype(jnp.float32)
    return result.reshape(tok_count, width_x).astype(jnp.bfloat16)


def solution(mesh):
    return jax.shard_map(
        body,
        mesh=mesh,
        in_specs=(
            P(("fsdp", "seq", "tp"), None),
            P(("fsdp", "seq"), "tp"),
            P(None, ("fsdp", "seq"), "tp"),
            P(("fsdp", "seq"), None, "tp"),
            P(None, ("fsdp", "seq"), None, "tp"),
            P(),
            P(("fsdp", "seq"), "tp"),
            P("tp"),
            P("tp"),
            P("tp"),
            P(None, "tp"),
            P(None, None, "tp"),
        ),
        out_specs=P(("fsdp", "seq"), "tp"),
        check_vma=False,
    )
```

profile of v0, /device:TPU:7, one launch (start us, length us, event | category | flops | bytes accessed | tf_op | source)
XLA Modules:
  0.0 569.9 jit_solution(6404143935002485496)
XLA Ops:
  11.3 5.7 fusion.10
  17.2 2.2 fusion
  22.1 20.0 %all_gather.19 = bf16[8192,32]{0,1:T(8,128)(2,1)S(1)} all-gather(bf16[512,32]{0,1:T(8,128)(2,1)S(1)} %copy-done.12), channel_id=1, replica_groups=mesh['fsdp'=2,'seq'=8,'tp'=2] {'fsdp','seq'}, dimensions={0}, use_global_device_ids=true | all-gather | bytes 557056 | tf_op jit(solution)/shard_map/all_gather | solution.py:74
  42.1 27.6 %all-gather.7.cloned.1.call-done = bf16[256,8192]{1,0:T(8,128)(2,1)} async-done(((bf16[128,8192]{1,0:T(8,128)(2,1)}), bf16[256,8192]{1,0:T(8,128)(2,1)}) %all-gather.7.cloned.1.call-update) | async-done | bytes 4194320 | tf_op jit(solution)/shard_map/all_gather | solution.py:61
  69.7 3.6 compare_select_fusion
  74.9 347.5 %all-gather.5.cloned.1.call-done = bf16[8192,3072]{1,0:T(8,128)(2,1)} async-done(((bf16[512,3072]{1,0:T(8,128)(2,1)}), bf16[8192,3072]{1,0:T(8,128)(2,1)}) %all-gather.5.cloned.1.call-update) | async-done | bytes 50331664 | tf_op jit(solution)/shard_map/all_gather | solution.py:68
  422.5 22.0 %fusion.1 = bf16[256,3072]{1,0:T(8,128)(2,1)S(1)} fusion(bf16[256,8192]{1,0:T(8,128)(2,1)} %all-gather.7.cloned.1.call-done, bf16[8192,3072]{1,0:T(8,128)(2,1)} %all-gather.5.cloned.1.call-done), kind=kOutput, calls=%fused_computation.10 | convolution fusion | flops 12885688320 | bytes 56098816 | tf_op jit(solution)/shard_map/dot_general | solution.py:66
  448.0 1.9 multiply_convert_fusion.1
  450.8 2.2 reshape.95
  453.0 2.2 copy.55
  461.1 10.8 %all-gather = f32[8,1,32]{2,1,0:T(1,128)S(1)} all-gather(f32[1,1,32]{2,1,0:T(1,128)S(1)} %get-tuple-element.87), channel_id=1, replica_groups=mesh['fsdp'=2,'seq'=8,'tp'=2] {'seq'}, dimensions={0}, use_global_device_ids=true | all-gather | bytes 1152 | tf_op jit(solution)/shard_map/all_gather | solution.py:20
  472.8 3.3 fusion.8
  476.1 38.8 %all-gather.9.cloned.1.call-done = f32[8,32,128,64]{2,3,1,0:T(8,128)} async-done(((f32[1,32,128,64]{2,3,1,0:T(8,128)}), f32[8,32,128,64]{2,3,1,0:T(8,128)}) %all-gather.9.cloned.1.call-update) | async-done | bytes 8388624 | tf_op jit(solution)/shard_map/all_gather | solution.py:20
  516.5 35.6 %while.12 = (s32[]{:T(128)}, f32[32,128,64]{2,1,0:T(8,128)}, s32[]{:T(128)}, f32[8,32]{1,0:T(8,128)S(1)}, f32[8,32,128,64]{2,3,1,0:T(8,128)}, /*index=5*/s32[]{:T(128)}, s32[]{:T(128)}, s32[]{:T(128)}) while((s32[]{:T(128)}, f32[32,128,64]{2,1,0:T(8,128)}, s32[]{:T(128)}, f32[8,32]{1,0:T(8,128)S(1)}, f32[8,32,128,64]{2,3,1,0:T(8,128)}, ...), condition=%wide.region_2.3_spmd, body=%wide.region_1.2_spmd.sunk | while | flops 524293 | bytes 7340543 | solution.py:28
  518.4 3.2 bitcast_add_fusion.11
  523.5 3.2 bitcast_add_fusion.11
  528.6 3.2 bitcast_add_fusion.11
  533.7 3.2 bitcast_add_fusion.11
  538.8 3.2 bitcast_add_fusion.11
  543.9 3.2 bitcast_add_fusion.11
  549.0 3.2 bitcast_add_fusion.11
  552.1 2.3 copy.62
  558.0 3.0 copy.67
  560.9 2.4 reshape.94
  (102 shorter events, 36.1 us)
Async XLA Ops:
  6.5 63.2 %all-gather.7.cloned.1.call-start = ((), (), s32[]{:S(2)}) async-start(), calls=%async_computation.1 | async-start | bytes 6291456 | tf_op jit(solution)/shard_map/all_gather | solution.py:61
  6.5 10.7 %copy-start.5 = (bf16[512,2048]{1,0:T(8,128)(2,1)S(1)}, bf16[512,2048]{1,0:T(8,128)(2,1)}, u32[]{:S(2)}) copy-start(bf16[512,2048]{1,0:T(8,128)(2,1)} %param.15) | copy-start | bytes 6291460
  7.3 415.2 %all-gather.5.cloned.1.call-start = ((), (), s32[]{:S(2)}) async-start(), calls=%async_computation | async-start | bytes 53477376 | tf_op jit(solution)/shard_map/all_gather | solution.py:68
  11.3 5.9 %copy-start.4 = (bf16[4,512,2048]{2,1,0:T(8,128)(2,1)S(1)}, bf16[4,512,2048]{2,1,0:T(8,128)(2,1)}, u32[]{:S(2)}) copy-start(bf16[4,512,2048]{2,1,0:T(8,128)(2,1)} %param.16) | copy-start | bytes 25165828
  21.3 0.7 copy-start.14
  21.3 0.8 copy-start.13
  21.3 0.8 copy-start.12
  21.3 48.4 %copy-start.15 = (f32[32]{0:T(128)S(1)}, f32[32]{0:T(128)}, u32[]{:S(2)}) copy-start(f32[32]{0:T(128)} %param.21) | copy-start | bytes 388
  21.4 52.7 %copy-start.17 = (f32[32]{0:T(128)S(1)}, f32[32]{0:T(128)}, u32[]{:S(2)}) copy-start(f32[32]{0:T(128)} %param.22) | copy-start | bytes 388
  21.4 493.6 %all-gather.9.cloned.1.call-start = ((), (), s32[]{:S(2)}) async-start(), calls=%async_computation.2 | async-start | bytes 9437184 | tf_op jit(solution)/shard_map/all_gather | solution.py:20
  73.3 0.6 copy-start.8
  444.5 3.1 collective-permute-start
  455.2 17.6 %copy-start.2 = (bf16[2,128,32,64]{1,3,2,0:T(8,128)(2,1)}, bf16[2,128,32,64]{1,3,2,0:T(8,128)(2,1)S(1)}, u32[]{:S(2)}) copy-start(bf16[2,128,32,64]{1,3,2,0:T(8,128)(2,1)S(1)} %copy.55) | copy-start | bytes 3145732
  455.2 1.8 copy-start.11
  457.7 1.4 copy-start
  457.7 2.6 copy-start.9
  457.7 2.7 copy-start.7
  552.1 2.4 copy-start.1
  554.5 1.2 copy-start.3
  554.5 1.9 copy-start.6
  554.5 1.9 copy-start.10
  554.5 1.9 copy-start.16
Sparse Core Ops, SparseCore 0:
  8.9 60.7 all-gather.6
  72.0 350.4 all-gather.4
  460.4 54.5 all-gather.8
where the time goes:
time: 571 us; the launch traced here: 570 us
  waiting for transfers between devices  416 us (73%)
  local copies, waits for them, and re-layouts  37.8 us (7%)
  other arithmetic  36.7 us (6%)
  matrix products  31.4 us (5%)
  blocking collectives  30.8 us (5%)
  between operations  16 us (3%)
    all_gather x1, waiting for transfers between devices, body(): lax.all_gather(weight_all, ('fsdp', 'seq'), axis=0, tiled=True)  348 us
    all_gather x1, waiting for transfers between devices, prefix(): gathered = jax.tree.map(lambda a: lax.all_gather(a, axis), part)  38.8 us
    all_gather x1, waiting for transfers between devices, body(): rows_all = lax.all_gather(tokens, 'tp', axis=0, tiled=True)  27.6 us
    add x8, other arithmetic, combine(): latter[0][:, None, None] * former[1] + latter[1]  23.3 us
    dot_general x1, matrix products, body(): jnp.dot(rows_all, lax.all_gather(weight_all, ('fsdp', 'seq'), axis=0, til...  22 us
    all_gather x1, blocking collectives, body(): lax.all_gather(dt_weight, ('fsdp', 'seq'), axis=0, tiled=True)  20 us
    dynamic_slice x14, local copies, waits for them, and re-layouts, one(): lax.dynamic_index_in_dim(a, hop, 0, False)  13.3 us
  transfers between devices with their start and end apart: 4, of which 4 were waited for; matrix products, arithmetic and copies ran while one was open for 4% of the time, Pallas kernels for 0%

commit v1 on v0

v1 whole, which is shorter than its diff:
```python
import jax
import jax.numpy as jnp
from jax import lax
from jax.sharding import Mesh, PartitionSpec as P

P_SIZE = 64
N = 128
CONV = 4
SPAN = 128
LANES = 128
SEQ = ("chip", "core")


def swapped(part, axis):
    return lax.ppermute(part, axis, [(0, 1), (1, 0)])


def sampled(mean_part, dev_part, swag_coef):
    factor = (2.0 * (dev_part.shape[0] - 1)) ** (-0.5)
    accum = mean_part.astype(jnp.float32)
    for member in range(dev_part.shape[0]):
        accum = accum + factor * swag_coef[member] * dev_part[member].astype(jnp.float32)
    return accum.astype(jnp.bfloat16)


def split_two(wide):
    high = lax.reduce_precision(wide, 8, 7)
    return high.astype(jnp.bfloat16), (wide - high).astype(jnp.bfloat16)


def narrowed(part, width, heads_here):
    body_part = part[:, :width].astype(jnp.bfloat16)
    if part.shape[1] == width:
        return body_part
    high, low = split_two(part[:, width : width + heads_here])
    fill = jnp.zeros((part.shape[0], part.shape[1] - width - 2 * heads_here), jnp.bfloat16)
    return jnp.concatenate([body_part, high, low, fill], axis=1)


def widened(part, width, heads_here):
    wide = part.astype(jnp.float32)
    if part.shape[1] == width:
        return wide
    logits = wide[:, width : width + heads_here] + wide[:, width + heads_here : width + 2 * heads_here]
    fill = jnp.zeros((part.shape[0], part.shape[1] - width - heads_here), jnp.float32)
    return jnp.concatenate([wide[:, :width], logits, fill], axis=1)


def gathered_rows(part):
    if lax.axis_size("tp") == 2:
        return jnp.concatenate([part, swapped(part, "tp")], axis=1)
    return lax.all_gather(part, "tp", axis=1, tiled=True)


def in_order(rows):
    if lax.axis_size("tp") != 2:
        return rows
    half = rows.shape[0] // 2
    flipped = jnp.concatenate([rows[half:], rows[:half]], axis=0)
    return jnp.where(lax.axis_index("tp") == 0, rows, flipped)


def prefix_decays(decay):
    place = lax.axis_index(SEQ)
    count = lax.axis_size(SEQ)
    before = jnp.ones_like(decay)
    total = decay
    levels = []
    by = 1
    while by < count:
        other = lax.ppermute(total, SEQ, [(i, i ^ by) for i in range(count)])
        upper = (place & by) != 0
        levels.append((upper, before, total, other))
        before = jnp.where(upper, other * before, before)
        total = total * other
        by *= 2
    return levels


def prefix_states(state, levels, part):
    count = lax.axis_size(SEQ)
    before = jnp.zeros_like(state)
    total = state
    by = 1
    for upper, before_decay, total_decay, other_decay in levels:
        other = lax.ppermute(
            total.astype(jnp.bfloat16), SEQ, [(i, i ^ by) for i in range(count)]
        ).astype(jnp.float32)
        before_decay, total_decay, other_decay = (
            d[part][:, None, None] for d in (before_decay, total_decay, other_decay)
        )
        before = before + jnp.where(upper, before_decay, 0.0) * other
        total = jnp.where(upper, total_decay * other + total, other_decay * total + other)
        by *= 2
    return before


def body(
    tokens,
    proj_mean,
    proj_devs,
    bc_mean,
    bc_devs,
    swag_coef,
    dt_weight,
    dt_bias,
    decay_rate,
    skip_gain,
    conv_proj,
    conv_bc,
):
    heads_here = decay_rate.shape[0]
    groups_here = bc_mean.shape[2] // N
    per_group = heads_here // groups_here
    width_x = proj_mean.shape[1]
    width_bc = 2 * bc_mean.shape[2]
    rows_k = proj_mean.shape[0]
    f_at, c_at = lax.axis_index("fsdp"), lax.axis_index("core")

    shares = tokens.reshape(tokens.shape[0], 2, -1, 2, rows_k)
    pick = lambda a, at, axis: lax.dynamic_index_in_dim(a, at, axis, keepdims=False)
    half_kept, half_sent = pick(shares, f_at, 1), pick(shares, 1 - f_at, 1)

    def rows_of(half):
        kept = pick(half, c_at, 2).reshape(1, tokens.shape[0], -1)
        sent = pick(half, 1 - c_at, 2).reshape(1, tokens.shape[0], -1)
        both = jnp.concatenate([kept, swapped(sent, "core")], axis=0)
        both = gathered_rows(both)
        return both.reshape(-1, both.shape[2])

    half_got = swapped(half_sent, "fsdp")
    rows_own = rows_of(half_kept)
    rows_other = rows_of(half_got)
    tok_count = rows_own.shape[0] // 2

    def projected(weight, width):
        whole = lax.all_gather(weight, "chip", axis=0, tiled=True)
        part_other = jnp.dot(rows_other, whole, preferred_element_type=jnp.float32)
        part_own = jnp.dot(rows_own, whole, preferred_element_type=jnp.float32)
        sent = jnp.concatenate([part_other[tok_count:], part_own[tok_count:]], axis=0)
        got = widened(swapped(narrowed(sent, width, heads_here), "core"), width, heads_here)
        back = part_other[:tok_count] + got[:tok_count]
        back = widened(swapped(narrowed(back, width, heads_here), "fsdp"), width, heads_here)
        return in_order(part_own[:tok_count] + got[tok_count:] + back)

    def convolved(proj, kernel):
        proj = proj.astype(jnp.bfloat16)
        count = lax.axis_size(SEQ)
        rim = lax.ppermute(
            proj[tok_count - (CONV - 1) :], SEQ, [(i, i + 1) for i in range(count - 1)]
        )
        padded = jnp.concatenate([rim, proj], axis=0).astype(jnp.float32)
        conv_sum = kernel[0] * padded[0:tok_count]
        for offset in range(1, CONV):
            conv_sum = conv_sum + kernel[offset] * padded[offset : offset + tok_count]
        return jax.nn.silu(conv_sum).astype(jnp.bfloat16)

    blocks = tok_count // SPAN
    fill = -heads_here % LANES
    weight_bc = sampled(bc_mean, bc_devs, swag_coef).reshape(rows_k, width_bc)
    weight_bc = jnp.concatenate([weight_bc, dt_weight, jnp.zeros((rows_k, fill), jnp.bfloat16)], axis=1)
    proj_bc = projected(weight_bc, width_bc)
    step_size = jax.nn.softplus(proj_bc[:, width_bc : width_bc + heads_here] + dt_bias)
    steps_b = step_size.reshape(blocks, SPAN, heads_here)
    cum_log = jnp.cumsum(-steps_b * decay_rate, axis=1)
    last_cum = cum_log[:, SPAN - 1 :, :]
    block_decay = jnp.exp(last_cum[:, 0, :])
    levels = prefix_decays(jnp.exp(jnp.sum(last_cum[:, 0, :], axis=0)))
    conv_out = convolved(proj_bc[:, :width_bc], conv_bc.reshape(CONV, width_bc))
    keys_b = conv_out[:, : width_bc // 2].reshape(blocks, SPAN, groups_here, N)
    reads_c = conv_out[:, width_bc // 2 :].reshape(blocks, SPAN, groups_here, N)
    scores = jnp.einsum("bqgn,bsgn->bgqs", reads_c, keys_b, preferred_element_type=jnp.float32)
    causal_mask = jnp.tril(jnp.ones((SPAN, SPAN), bool))

    def finished(first, group_count):
        heads = group_count * per_group
        part = slice(first * per_group, first * per_group + heads)
        cols = slice(part.start * P_SIZE, part.stop * P_SIZE)
        weight_x = sampled(proj_mean[:, cols], proj_devs[:, :, cols], swag_coef)
        values = convolved(projected(weight_x, heads * P_SIZE), conv_proj[:, cols])
        values = values.reshape(blocks, SPAN, heads, P_SIZE)
        cum, steps = cum_log[:, :, part], steps_b[:, :, part]
        scaled = (
            values.astype(jnp.float32) * (jnp.exp(last_cum[:, :, part] - cum) * steps)[..., None]
        ).astype(jnp.bfloat16)
        keys_h = jnp.repeat(keys_b[:, :, first : first + group_count], per_group, axis=2)
        reads_h = jnp.repeat(reads_c[:, :, first : first + group_count], per_group, axis=2)
        states = jnp.einsum("bshn,bshp->bhnp", keys_h, scaled, preferred_element_type=jnp.float32)
        decay = block_decay[:, part]
        total_state = states[0]
        for member in range(1, blocks):
            total_state = decay[member][:, None, None] * total_state + states[member]
        carried = prefix_states(total_state, levels, part)
        later_cum = jnp.transpose(cum, (0, 2, 1))
        cum_gaps = later_cum[:, :, :, None] - later_cum[:, :, None, :]
        decays = jnp.where(causal_mask, jnp.exp(jnp.minimum(cum_gaps, 0.0)), 0.0)
        scores_h = jnp.repeat(scores[:, first : first + group_count], per_group, axis=1)
        weights = (scores_h * decays * jnp.transpose(steps, (0, 2, 1))[:, :, None, :]).astype(jnp.bfloat16)
        inner_part = jnp.einsum("bhqs,bshp->bqhp", weights, values, preferred_element_type=jnp.float32)
        entering = []
        for member in range(blocks):
            entering.append(carried)
            carried = decay[member][:, None, None] * carried + states[member]
        entering_bf = jnp.stack(entering).astype(jnp.bfloat16)
        outer_part = jnp.exp(cum)[..., None] * jnp.einsum(
            "bqhn,bhnp->bqhp", reads_h, entering_bf, preferred_element_type=jnp.float32
        )
        result = inner_part + outer_part + skip_gain[part, None] * values.astype(jnp.float32)
        return result.reshape(tok_count, heads * P_SIZE).astype(jnp.bfloat16)

    at_once = max(1, groups_here // 2)
    pieces = [finished(first, at_once) for first in range(0, groups_here, at_once)]
    return jnp.concatenate(pieces, axis=1)


def solution(mesh):
    shape = mesh.shape
    split = Mesh(
        mesh.devices.reshape(shape["fsdp"], shape["seq"] // 2, 2, shape["tp"]),
        ("fsdp", "chip", "core", "tp"),
    )
    rows = ("fsdp", "chip", "core")
    return jax.shard_map(
        body,
        mesh=split,
        in_specs=(
            P(rows + ("tp",), None),
            P(rows, "tp"),
            P(None, rows, "tp"),
            P(rows, None, "tp"),
            P(None, rows, None, "tp"),
            P(),
            P(rows, "tp"),
            P("tp"),
            P("tp"),
            P("tp"),
            P(None, "tp"),
            P(None, None, "tp"),
        ),
        out_specs=P(rows, "tp"),
        check_vma=False,
    )
```

time: 571 us -> 351 us (0.61)
  the two profiles are of different devices: /device:TPU:7 before, /device:TPU:0 now
where the time goes in v1:
time: 351 us; the launch traced here: 344 us
  waiting for transfers between devices  186 us (53%)
  other arithmetic  45.6 us (13%)
  local copies, waits for them, and re-layouts  40.9 us (12%)
  matrix products  31.2 us (9%)
  starting transfers between devices  23.1 us (7%)
  between operations  17.2 us (5%)
    ppermute x11, waiting for transfers between devices, swapped(): return lax.ppermute(part, axis, [(0, 1), (1, 0)])  148 us
    all_gather x3, waiting for transfers between devices, projected(): whole = lax.all_gather(weight, 'chip', axis=0, tiled=True)  26.9 us
    dot_general x3, matrix products, projected(): part_other = jnp.dot(rows_other, whole, preferred_element_type=jnp.float32)  17.2 us
    unnamed x98, local copies, waits for them, and re-layouts  11.8 us
    convert_element_type x2, other arithmetic, sampled(): return accum.astype(jnp.bfloat16)  11.6 us
    ppermute x11, starting transfers between devices, swapped(): return lax.ppermute(part, axis, [(0, 1), (1, 0)])  9.76 us
    ppermute x6, waiting for transfers between devices, prefix_states(): lax.ppermute(total.astype(jnp.bfloat16), SEQ, [(i, i ^ by) for i in range...  9.67 us
    dot_general x3, matrix products, projected(): part_own = jnp.dot(rows_own, whole, preferred_element_type=jnp.float32)  7.47 us
  transfers between devices with their start and end apart: 25, of which 12 were waited for; matrix products, arithmetic and copies ran while one was open for 26% of the time, Pallas kernels for 0%

profile of v1, /device:TPU:0, one launch (start us, length us, event | category | flops | bytes accessed | tf_op | source)
XLA Modules:
  0.0 344.3 jit_solution(225934653815547059)
XLA Ops:
  10.5 6.2 %fusion.4 = (bf16[512,1024]{1,0:T(8,128)(2,1)}, bf16[512,1024]{1,0:T(8,128)(2,1)}) fusion(bf16[4,512,2048]{2,1,0:T(8,128)(2,1)} %param.14, f32[]{:T(128)} %bitcast.11, f32[]{:T(128)} %bitcast.9, f32[]{:T(128)} %bitcast.7, f32[]{:T(128)} %bitcast.5, bf16[512,2048]{1,0:T(8,128)(2,1)} %param.13), kind=kLoop, calls=%fused_computation.18 | loop fusion | flops 14680064 | bytes 12582928 | tf_op jit(solution)/shard_map/convert_element_type | solution.py:23
  18.0 5.3 %fusion.3 = bf16[512,2,512]{2,1,0:T(2,128)(2,1)S(1)} fusion(bf16[512,2,512]{2,1,0:T(2,128)(2,1)S(1)} %copy-done.19, bf16[4,512,2,512]{3,2,1,0:T(2,128)(2,1)} %param.16, f32[]{:T(128)} %bitcast.11, f32[]{:T(128)} %bitcast.9, f32[]{:T(128)} %bitcast.7, f32[]{:T(128)} %bitcast.5), kind=kLoop, calls=%fused_computation.13 | loop fusion | flops 7340032 | bytes 6291472 | tf_op jit(solution)/shard_map/convert_element_type | solution.py:23
  26.2 3.3 copy.121
  30.9 4.0 %collective-permute-start.2 = (bf16[128,4,2,512]{3,0,2,1:T(8,128)(2,1)}, bf16[128,4,2,512]{3,0,2,1:T(8,128)(2,1)}, u32[]{:S(2)}, u32[]{:S(2)}) collective-permute-start(bf16[128,4,2,512]{3,0,2,1:T(8,128)(2,1)} %bitcast.245), channel_id=1, source_target_pairs={{0,16},{16,0},{1,17},{17,1},{2,18},{18,2},{3,19},{19,3},{4,20},{20... | collective-permute-start | bytes 3145736 | tf_op jit(solution)/shard_map/ppermute | solution.py:15
  35.1 45.8 %collective-permute-done.2 = bf16[128,4,2,512]{3,0,2,1:T(8,128)(2,1)} collective-permute-done((bf16[128,4,2,512]{3,0,2,1:T(8,128)(2,1)}, bf16[128,4,2,512]{3,0,2,1:T(8,128)(2,1)}, u32[]{:S(2)}, u32[]{:S(2)}) %collective-permute-start.2) | collective-permute-done | bytes 1048608 | tf_op jit(solution)/shard_map/ppermute | solution.py:15
  88.3 21.8 %collective-permute-done.1 = bf16[2,128,2048]{1,2,0:T(8,128)(2,1)} collective-permute-done((bf16[2,128,2048]{1,2,0:T(8,128)(2,1)}, bf16[2,128,2048]{1,2,0:T(8,128)(2,1)}, u32[]{:S(2)}, u32[]{:S(2)}) %collective-permute-start.1) | collective-permute-done | bytes 1048608 | tf_op jit(solution)/shard_map/ppermute | solution.py:15
  111.7 2.5 copy.122
  114.2 18.0 %collective-permute-done.4 = bf16[2,128,2048]{1,2,0:T(8,128)(2,1)} collective-permute-done((bf16[2,128,2048]{1,2,0:T(8,128)(2,1)}, bf16[2,128,2048]{1,2,0:T(8,128)(2,1)}, u32[]{:S(2)}, u32[]{:S(2)}) %collective-permute-start.4) | collective-permute-done | bytes 1048608 | tf_op jit(solution)/shard_map/ppermute | solution.py:15
  133.7 2.6 copy.127
  136.3 5.8 %fusion.111 = f32[512,1024]{0,1:T(8,128)S(1)} fusion(bf16[512,2048]{1,0:T(8,128)(2,1)} %bitcast.238, bf16[2048,1024]{1,0:T(8,128)(2,1)} %all-gather.4.cloned.1.call-done), kind=kOutput, calls=%fused_computation.232 | convolution fusion | flops 2147483648 | bytes 8388608 | tf_op jit(solution)/shard_map/dot_general | solution.py:138
  143.5 2.4 fusion.110
  147.6 5.3 %fusion.115 = f32[512,1024]{0,1:T(8,128)S(1)} fusion(bf16[512,2048]{1,0:T(8,128)(2,1)} %bitcast.239, bf16[2048,1024]{1,0:T(8,128)(2,1)} %all-gather.8.cloned.1.call-done), kind=kOutput, calls=%fused_computation.236 | convolution fusion | flops 2147483648 | bytes 8388608 | tf_op jit(solution)/shard_map/dot_general | solution.py:138
  154.4 2.4 fusion.114
  159.0 26.9 %all-gather.6.cloned.1.call-done = bf16[2048,1152]{1,0:T(8,128)(2,1)} async-done(((bf16[512,1152]{1,0:T(8,128)(2,1)}), bf16[2048,1152]{1,0:T(8,128)(2,1)}) %all-gather.6.cloned.1.call-update) | async-done | bytes 4718608 | tf_op jit(solution)/shard_map/all_gather | solution.py:137
  185.9 6.0 %fusion.113 = f32[512,1152]{0,1:T(8,128)S(1)} fusion(bf16[512,2048]{1,0:T(8,128)(2,1)} %bitcast.240, bf16[2048,1152]{1,0:T(8,128)(2,1)} %all-gather.6.cloned.1.call-done), kind=kOutput, calls=%fused_computation.234 | convolution fusion | flops 2415919104 | bytes 9175040 | tf_op jit(solution)/shard_map/dot_general | solution.py:138
  192.0 2.7 fusion.112
  198.3 2.5 collective-permute-start.6
  203.5 32.9 %collective-permute-done.6 = bf16[256,1024]{0,1:T(8,128)(2,1)S(1)} collective-permute-done((bf16[256,1024]{0,1:T(8,128)(2,1)S(1)}, bf16[256,1024]{0,1:T(8,128)(2,1)S(1)}, u32[]{:S(2)}, u32[]{:S(2)}) %collective-permute-start.6) | collective-permute-done | bytes 524320 | tf_op jit(solution)/shard_map/ppermute | solution.py:15
  238.4 8.2 %collective-permute-done.17 = bf16[256,1024]{0,1:T(8,128)(2,1)S(1)} collective-permute-done((bf16[256,1024]{0,1:T(8,128)(2,1)S(1)}, bf16[256,1024]{0,1:T(8,128)(2,1)S(1)}, u32[]{:S(2)}, u32[]{:S(2)}) %collective-permute-start.17) | collective-permute-done | bytes 524320 | tf_op jit(solution)/shard_map/ppermute | solution.py:15
  257.3 2.3 multiply_convert_fusion.4
  260.8 21.4 %collective-permute-done.9 = bf16[256,1152]{0,1:T(8,128)(2,1)} collective-permute-done((bf16[256,1152]{0,1:T(8,128)(2,1)}, bf16[256,1152]{0,1:T(8,128)(2,1)}, u32[]{:S(2)}, u32[]{:S(2)}) %collective-permute-start.9) | collective-permute-done | bytes 589856 | tf_op jit(solution)/shard_map/ppermute | solution.py:15
  287.5 2.4 collective-permute-start.10
  312.6 5.9 %collective-permute-done.13 = bf16[16,128,64]{1,2,0:T(8,128)(2,1)S(1)} collective-permute-done((bf16[16,128,64]{1,2,0:T(8,128)(2,1)S(1)}, bf16[16,128,64]{1,2,0:T(8,128)(2,1)S(1)}, u32[]{:S(2)}, u32[]{:S(2)}) %collective-permute-start.13) | collective-permute-done | bytes 262176 | tf_op jit(solution)/shard_map/ppermute | solution.py:86
  330.2 2.6 collective-permute-done.21
  (260 shorter events, 87.8 us)
Async XLA Ops:
  6.5 129.8 %all-gather.4.cloned.1.call-start = ((), (), s32[]{:S(2)}) async-start(), calls=%async_computation | async-start | bytes 5242880 | tf_op jit(solution)/shard_map/all_gather | solution.py:137
  16.8 130.9 %all-gather.8.cloned.1.call-start = ((), (), s32[]{:S(2)}) async-start(), calls=%async_computation.2 | async-start | bytes 5242880 | tf_op jit(solution)/shard_map/all_gather | solution.py:137
  17.5 168.3 %all-gather.6.cloned.1.call-start = ((), (), s32[]{:S(2)}) async-start(), calls=%async_computation.1 | async-start | bytes 5898240 | tf_op jit(solution)/shard_map/all_gather | solution.py:137
  30.9 49.9 %collective-permute-start.2 = (bf16[128,4,2,512]{3,0,2,1:T(8,128)(2,1)}, bf16[128,4,2,512]{3,0,2,1:T(8,128)(2,1)}, u32[]{:S(2)}, u32[]{:S(2)}) collective-permute-start(bf16[128,4,2,512]{3,0,2,1:T(8,128)(2,1)} %bitcast.245), channel_id=1, source_target_pairs={{0,16},{16,0},{1,17},{17,1},{2,18},{18,2},{3,19},{19,3},{4,20},{20... | collective-permute-start | bytes 3145736 | tf_op jit(solution)/shard_map/ppermute | solution.py:15
  35.0 47.7 %collective-permute-start = (bf16[1,128,2048]{1,2,0:T(8,128)(2,1)S(1)}, bf16[1,128,2048]{1,2,0:T(8,128)(2,1)S(1)}, u32[]{:S(2)}, u32[]{:S(2)}) collective-permute-start(bf16[1,128,2048]{1,2,0:T(8,128)(2,1)S(1)} %bitcast.247), channel_id=1, source_target_pairs={{0,2},{2,0},{1,3},{3,1},{4,6},{6,4},{5,7},{7,5},{8,10},{10,8},{9,1... | collective-permute-start | bytes 1572872 | tf_op jit(solution)/shard_map/ppermute | solution.py:15
  83.9 26.3 %collective-permute-start.1 = (bf16[2,128,2048]{1,2,0:T(8,128)(2,1)}, bf16[2,128,2048]{1,2,0:T(8,128)(2,1)}, u32[]{:S(2)}, u32[]{:S(2)}) collective-permute-start(bf16[2,128,2048]{1,2,0:T(8,128)(2,1)} %pad_maximum_fusion.2), channel_id=1, source_target_pairs={{0,1},{1,0},{2,3},{3,2},{4,5},{5,4},{6,7},{7,6},{8,9},{9,8},{10,11... | collective-permute-start | bytes 3145736 | tf_op jit(solution)/shard_map/ppermute | solution.py:15
  86.1 46.1 %collective-permute-start.4 = (bf16[2,128,2048]{1,2,0:T(8,128)(2,1)}, bf16[2,128,2048]{1,2,0:T(8,128)(2,1)}, u32[]{:S(2)}, u32[]{:S(2)}) collective-permute-start(bf16[2,128,2048]{1,2,0:T(8,128)(2,1)} %pad_maximum_fusion.3), channel_id=1, source_target_pairs={{0,1},{1,0},{2,3},{3,2},{4,5},{5,4},{6,7},{7,6},{8,9},{9,8},{10,11... | collective-permute-start | bytes 3145736 | tf_op jit(solution)/shard_map/ppermute | solution.py:15
  147.6 48.5 %collective-permute-start.5 = (bf16[512,1024]{0,1:T(8,128)(2,1)}, bf16[512,1024]{0,1:T(8,128)(2,1)}, u32[]{:S(2)}, u32[]{:S(2)}) collective-permute-start(bf16[512,1024]{0,1:T(8,128)(2,1)} %pad_maximum_fusion.4), channel_id=1, source_target_pairs={{0,2},{2,0},{1,3},{3,1},{4,6},{6,4},{5,7},{7,5},{8,10},{10,8},{9,1... | collective-permute-start | bytes 3145736 | tf_op jit(solution)/shard_map/ppermute | solution.py:15
  158.5 42.7 %collective-permute-start.16 = (bf16[512,1024]{0,1:T(8,128)(2,1)}, bf16[512,1024]{0,1:T(8,128)(2,1)S(1)}, u32[]{:S(2)}, u32[]{:S(2)}) collective-permute-start(bf16[512,1024]{0,1:T(8,128)(2,1)} %pad_maximum_fusion.5), channel_id=1, source_target_pairs={{0,2},{2,0},{1,3},{3,1},{4,6},{6,4},{5,7},{7,5},{8,10},{10,8},{9,1... | collective-permute-start | bytes 3145736 | tf_op jit(solution)/shard_map/ppermute | solution.py:15
  198.3 38.1 %collective-permute-start.6 = (bf16[256,1024]{0,1:T(8,128)(2,1)S(1)}, bf16[256,1024]{0,1:T(8,128)(2,1)S(1)}, u32[]{:S(2)}, u32[]{:S(2)}) collective-permute-start(bf16[256,1024]{0,1:T(8,128)(2,1)S(1)} %fusion.27), channel_id=1, source_target_pairs={{0,16},{16,0},{1,17},{17,1},{2,18},{18,2},{3,19},{19,3},{4,20},{20... | collective-permute-start | bytes 1572872 | tf_op jit(solution)/shard_map/ppermute | solution.py:15
  201.1 49.2 %collective-permute-start.8 = (bf16[512,1152]{0,1:T(8,128)(2,1)S(1)}, bf16[512,1152]{0,1:T(8,128)(2,1)S(1)}, u32[]{:S(2)}, u32[]{:S(2)}) collective-permute-start(bf16[512,1152]{0,1:T(8,128)(2,1)S(1)} %maximum_maximum_fusion.1), channel_id=1, source_target_pairs={{0,2},{2,0},{1,3},{3,1},{4,6},{6,4},{5,7},{7,5},{8,10},{10,8},{9,1... | collective-permute-start | bytes 3538952 | tf_op jit(solution)/shard_map/ppermute | solution.py:15
  203.0 43.7 %collective-permute-start.17 = (bf16[256,1024]{0,1:T(8,128)(2,1)S(1)}, bf16[256,1024]{0,1:T(8,128)(2,1)S(1)}, u32[]{:S(2)}, u32[]{:S(2)}) collective-permute-start(bf16[256,1024]{0,1:T(8,128)(2,1)S(1)} %fusion.19), channel_id=1, source_target_pairs={{0,16},{16,0},{1,17},{17,1},{2,18},{18,2},{3,19},{19,3},{4,20},{20... | collective-permute-start | bytes 1572872 | tf_op jit(solution)/shard_map/ppermute | solution.py:15
  237.0 12.9 %collective-permute-start.7 = (bf16[3,1024]{0,1:T(8,128)(2,1)S(1)}, bf16[3,1024]{0,1:T(8,128)(2,1)S(1)}, u32[]{:S(2)}, u32[]{:S(2)}) collective-permute-start(bf16[3,1024]{0,1:T(8,128)(2,1)S(1)} %slice.530), channel_id=1, source_target_pairs={{0,2},{2,4},{4,6},{6,8},{8,10},{10,12},{12,14},{1,3},{3,5},{5,7},{... | collective-permute-start | bytes 18440 | tf_op jit(solution)/shard_map/ppermute | solution.py:149
  247.9 8.1 %collective-permute-start.18 = (bf16[3,1024]{0,1:T(8,128)(2,1)}, bf16[3,1024]{0,1:T(8,128)(2,1)}, u32[]{:S(2)}, u32[]{:S(2)}) collective-permute-start(bf16[3,1024]{0,1:T(8,128)(2,1)} %slice.579), channel_id=1, source_target_pairs={{0,2},{2,4},{4,6},{6,8},{8,10},{10,12},{12,14},{1,3},{3,5},{5,7},{... | collective-permute-start | bytes 18440 | tf_op jit(solution)/shard_map/ppermute | solution.py:149
  252.6 29.6 %collective-permute-start.9 = (bf16[256,1152]{0,1:T(8,128)(2,1)}, bf16[256,1152]{0,1:T(8,128)(2,1)}, u32[]{:S(2)}, u32[]{:S(2)}) collective-permute-start(bf16[256,1152]{0,1:T(8,128)(2,1)} %maximum_maximum_fusion.2), channel_id=1, source_target_pairs={{0,16},{16,0},{1,17},{17,1},{2,18},{18,2},{3,19},{19,3},{4,20},{20... | collective-permute-start | bytes 1769480 | tf_op jit(solution)/shard_map/ppermute | solution.py:15
  286.5 5.3 %collective-permute-start.12 = (f32[32]{0:T(128)S(1)}, f32[32]{0:T(128)S(1)}, u32[]{:S(2)}, u32[]{:S(2)}) collective-permute-start(f32[32]{0:T(128)S(1)} %exp.49), channel_id=1, source_target_pairs={{0,2},{2,0},{4,6},{6,4},{8,10},{10,8},{12,14},{14,12},{1,3},{3,1},... | collective-permute-start | bytes 392 | tf_op jit(solution)/shard_map/ppermute | solution.py:71
  287.5 9.3 %collective-permute-start.10 = (bf16[3,1024]{0,1:T(8,128)(2,1)S(1)}, bf16[3,1024]{0,1:T(8,128)(2,1)S(1)}, u32[]{:S(2)}, u32[]{:S(2)}) collective-permute-start(bf16[3,1024]{0,1:T(8,128)(2,1)S(1)} %slice.553), channel_id=1, source_target_pairs={{0,2},{2,4},{4,6},{6,8},{8,10},{10,12},{12,14},{1,3},{3,5},{5,7},{... | collective-permute-start | bytes 18440 | tf_op jit(solution)/shard_map/ppermute | solution.py:149
  291.8 3.7 %collective-permute-start.14 = (f32[32]{0:T(128)S(1)}, f32[32]{0:T(128)S(1)}, u32[]{:S(2)}, u32[]{:S(2)}) collective-permute-start(f32[32]{0:T(128)S(1)} %exponential_multiply_fusion.2), channel_id=1, source_target_pairs={{0,4},{2,6},{4,0},{6,2},{8,12},{10,14},{12,8},{14,10},{1,5},{3,7},... | collective-permute-start | bytes 392 | tf_op jit(solution)/shard_map/ppermute | solution.py:71
  300.7 7.4 %collective-permute-start.11 = (bf16[16,128,64]{1,2,0:T(8,128)(2,1)}, bf16[16,128,64]{1,2,0:T(8,128)(2,1)}, u32[]{:S(2)}, u32[]{:S(2)}) collective-permute-start(bf16[16,128,64]{1,2,0:T(8,128)(2,1)} %fusion.80), channel_id=1, source_target_pairs={{0,2},{2,0},{4,6},{6,4},{8,10},{10,8},{12,14},{14,12},{1,3},{3,1},... | collective-permute-start | bytes 786440 | tf_op jit(solution)/shard_map/ppermute | solution.py:86
  303.0 7.7 %collective-permute-start.19 = (bf16[16,128,64]{1,2,0:T(8,128)(2,1)S(1)}, bf16[16,128,64]{1,2,0:T(8,128)(2,1)S(1)}, u32[]{:S(2)}, u32[]{:S(2)}) collective-permute-start(bf16[16,128,64]{1,2,0:T(8,128)(2,1)S(1)} %fusion.81), channel_id=1, source_target_pairs={{0,2},{2,0},{4,6},{6,4},{8,10},{10,8},{12,14},{14,12},{1,3},{3,1},... | collective-permute-start | bytes 786440 | tf_op jit(solution)/shard_map/ppermute | solution.py:86
  309.3 9.2 %collective-permute-start.13 = (bf16[16,128,64]{1,2,0:T(8,128)(2,1)S(1)}, bf16[16,128,64]{1,2,0:T(8,128)(2,1)S(1)}, u32[]{:S(2)}, u32[]{:S(2)}) collective-permute-start(bf16[16,128,64]{1,2,0:T(8,128)(2,1)S(1)} %get-tuple-element.5), channel_id=1, source_target_pairs={{0,4},{2,6},{4,0},{6,2},{8,12},{10,14},{12,8},{14,10},{1,5},{3,7},... | collective-permute-start | bytes 786440 | tf_op jit(solution)/shard_map/ppermute | solution.py:86
  311.9 11.7 %collective-permute-start.20 = (bf16[16,128,64]{1,2,0:T(8,128)(2,1)}, bf16[16,128,64]{1,2,0:T(8,128)(2,1)}, u32[]{:S(2)}, u32[]{:S(2)}) collective-permute-start(bf16[16,128,64]{1,2,0:T(8,128)(2,1)} %get-tuple-element.9), channel_id=1, source_target_pairs={{0,4},{2,6},{4,0},{6,2},{8,12},{10,14},{12,8},{14,10},{1,5},{3,7},... | collective-permute-start | bytes 786440 | tf_op jit(solution)/shard_map/ppermute | solution.py:86
  319.5 7.5 %collective-permute-start.15 = (bf16[16,128,64]{1,2,0:T(8,128)(2,1)}, bf16[16,128,64]{1,2,0:T(8,128)(2,1)}, u32[]{:S(2)}, u32[]{:S(2)}) collective-permute-start(bf16[16,128,64]{1,2,0:T(8,128)(2,1)} %fusion.47), channel_id=1, source_target_pairs={{0,8},{2,10},{4,12},{6,14},{8,0},{10,2},{12,4},{14,6},{1,9},{3,11}... | collective-permute-start | bytes 786440 | tf_op jit(solution)/shard_map/ppermute | solution.py:86
  325.0 7.8 %collective-permute-start.21 = (bf16[16,128,64]{1,2,0:T(8,128)(2,1)S(1)}, bf16[16,128,64]{1,2,0:T(8,128)(2,1)S(1)}, u32[]{:S(2)}, u32[]{:S(2)}) collective-permute-start(bf16[16,128,64]{1,2,0:T(8,128)(2,1)S(1)} %fusion.54), channel_id=1, source_target_pairs={{0,8},{2,10},{4,12},{6,14},{8,0},{10,2},{12,4},{14,6},{1,9},{3,11}... | collective-permute-start | bytes 786440 | tf_op jit(solution)/shard_map/ppermute | solution.py:86
  (44 other events, 229.7 us)
Sparse Core Ops, SparseCore 0:
  16.9 55.3 all-gather.3
  74.2 52.6 all-gather.7
  128.8 57.0 all-gather.5
